TPU v7x, 256 devices: a whole 4x4x8 slice. The times are simulated.
256 devices in a mesh: dp: 32 (over x, z), tensor: 8 (over y, core).
Axes of the slice: x: 4, y: 4, z: 8, core: 2. Of those that a mesh axis runs over, the one named last changes fastest.
Arguments:
- tokens: bfloat16 [8192, 4096], P('dp', 'tensor'), may hold values from -17 to 17
- cotangent: bfloat16 [8192, 17408], P('dp', 'tensor'), may hold values from -6 to 6
- weight_blocks: bfloat16 [7168, 4096], P('tensor'), may hold values from -0.09375 to 0.09375
- block_rows: int32 [7168], P('tensor'), may hold values from 0 to 63, as said below
- block_slots: int32 [7168], P('tensor'), may hold values from 0 to 33, as said below
Outputs:
- hidden: bfloat16 [8192, 17408], P('dp', 'tensor')
- input_grads: bfloat16 [8192, 4096], P('dp', 'tensor')
- curvature: float32 [7168, 4096], P('tensor', 'dp')
Inputs may be any that keep to these rules, and one draw needn't show every extreme that they name: On each tensor device the pairs (block_slots, block_rows) of its 896 blocks are distinct and listed by slot, then by row. `block_slots`: A slot holds 0, 16 or 48 of its device's blocks; on half of the tensor devices every slot holds some.
All inputs are finite; a program needn't handle non-finite values.
Results may differ from a plain program's by a relative error of at most 0.013.
Values may be sent and summed in bfloat16 or wider, within the bound.
A program may use at most 320 MiB of HBM per device.

v0:
```python
import math

import jax
import jax.numpy as jnp
from jax import lax
from jax.sharding import PartitionSpec as P


def body(tokens, cotangent, weight_blocks, block_rows, block_slots):
    gathered = lax.all_gather(tokens, "tensor", axis=1, tiled=True)
    length = gathered.shape[0]
    block_size = math.isqrt(weight_blocks.shape[1])
    kept_count = weight_blocks.shape[0]
    slot_count = cotangent.shape[1] // block_size
    row_count = gathered.shape[1] // block_size
    pair_count = row_count * slot_count
    pair_keys = block_rows * slot_count + block_slots
    pair_range = jnp.arange(pair_count, dtype=jnp.int32)
    kept_range = jnp.arange(kept_count, dtype=jnp.int32)
    matches = pair_keys[None, :] == pair_range[:, None]
    present = jnp.any(matches, axis=1)
    position = jnp.sum(jnp.where(matches, kept_range[None, :], 0), axis=1)
    position = jnp.where(present, position, kept_count)
    padded_blocks = jnp.concatenate(
        [weight_blocks, jnp.zeros((1, block_size * block_size), weight_blocks.dtype)], axis=0
    )
    pair_blocks = jnp.take(padded_blocks, position, axis=0)
    dense_weight = pair_blocks.reshape(row_count, slot_count, block_size, block_size)
    dense_weight = dense_weight.transpose(0, 2, 1, 3).reshape(
        row_count * block_size, slot_count * block_size
    )
    hidden = jnp.dot(gathered, dense_weight, preferred_element_type=jnp.float32).astype(
        jnp.bfloat16
    )
    backward = lax.dot_general(
        cotangent, dense_weight, (((1,), (1,)), ((), ())), preferred_element_type=jnp.float32
    )
    input_grads = lax.psum_scatter(backward, "tensor", scatter_dimension=1, tiled=True).astype(
        jnp.bfloat16
    )
    squared_in = (gathered.astype(jnp.float32) * gathered.astype(jnp.float32)).astype(jnp.bfloat16)
    squared_back = (cotangent.astype(jnp.float32) * cotangent.astype(jnp.float32)).astype(
        jnp.bfloat16
    )
    half_rows = row_count // 2
    partial_value = jnp.zeros((kept_count, block_size * block_size), jnp.float32)
    for half in range(2):
        lower = half * half_rows * block_size
        square_part = squared_in[:, lower : lower + half_rows * block_size]
        outer = lax.dot_general(
            square_part, squared_back, (((0,), (0,)), ((), ())), preferred_element_type=jnp.float32
        )
        outer = outer.reshape(half_rows, block_size, slot_count, block_size).transpose(0, 2, 1, 3)
        outer = outer.reshape(half_rows * slot_count, block_size * block_size)
        local_key = pair_keys - half * half_rows * slot_count
        inside = (local_key >= 0) & (local_key < half_rows * slot_count)
        picked = jnp.take(outer, jnp.clip(local_key, 0, half_rows * slot_count - 1), axis=0)
        partial_value = jnp.where(inside[:, None], picked, partial_value)
    token_total = length * lax.axis_size("dp")
    curvature = lax.psum_scatter(
        partial_value.astype(jnp.bfloat16), "dp", scatter_dimension=1, tiled=True
    ).astype(jnp.float32)
    return (hidden, input_grads, curvature / token_total)


def solution(mesh):
    placed = (P("dp", "tensor"), P("dp", "tensor"), P("tensor", None), P("tensor"), P("tensor"))
    return jax.shard_map(
        body,
        mesh=mesh,
        in_specs=placed,
        out_specs=(P("dp", "tensor"), P("dp", "tensor"), P("tensor", "dp")),
        check_vma=False,
    )
```

profile of v0, /device:TPU:8, one launch (start us, length us, event | category | flops | bytes accessed | tf_op | source)
XLA Modules:
  0.0 698.7 jit_solution(7023754844757312933)
XLA Ops:
  7.2 0.7 all-gather.2.cloned.1.call-update
  7.9 1.3 compare_and_fusion.4
  9.2 0.9 fusion.2
  10.2 0.9 select_reduce_fusion
  11.2 7.0 %concatenate.3 = bf16[897,4096]{1,0:T(8,128)(2,1)} pad(bf16[896,4096]{1,0:T(8,128)(2,1)} %param.9, bf16[]{:T(256)} %constant.25.clone.1), padding=0_1x0_0 | pad | bytes 14688258 | tf_op jit(solution)/shard_map/concatenate | solution.py:24
  18.2 36.4 %gather_fusion = bf16[2176,4096]{1,0:T(8,128)(2,1)} fusion(bf16[897,4096]{1,0:T(8,128)(2,1)} %concatenate.3, s32[3072]{0:T(1024)S(1)} %pad_clamp_fusion), kind=kCustom, calls=%fused_computation.2 | custom fusion | bytes 35660288 | tf_op jit(solution)/shard_map/jit(_take)/gather | solution.py:27
  54.7 48.7 %gather.10 = bf16[64,34,64,64]{3,2,1,0:T(8,128)(2,1)} reshape(bf16[2176,4096]{1,0:T(8,128)(2,1)} %gather_fusion) | data formatting | bytes 35651584 | tf_op jit(solution)/shard_map/jit(_take)/gather | solution.py:27
  103.3 49.5 %copy.29 = bf16[64,34,64,64]{2,0,3,1:T(8,128)(2,1)} copy(bf16[64,34,64,64]{3,2,1,0:T(8,128)(2,1)} %gather.10) | data formatting | bytes 35651584 | tf_op jit(solution)/shard_map/jit(_take)/gather | solution.py:27
  153.0 24.1 %select_bitcast_fusion = bf16[64,64,34,64]{1,0,3,2:T(8,128)(2,1)} fusion(bf16[64,34,64,64]{2,0,3,1:T(8,128)(2,1)} %copy.29, pred[64,34]{0,1:T(8,128)(4,1)S(1)} %copy.28), kind=kLoop, calls=%fused_computation.3 | loop fusion | flops 8912896 | bytes 35653760 | tf_op jit(solution)/shard_map/transpose | solution.py:29
  177.1 46.7 %reshape.67 = bf16[4096,2176]{0,1:T(8,128)(2,1)} reshape(bf16[64,64,34,64]{1,0,3,2:T(8,128)(2,1)} %select_bitcast_fusion) | data formatting | bytes 35651584 | tf_op jit(solution)/shard_map/reshape | solution.py:29
  223.8 10.3 %convolution_bitcast_fusion = f32[256,4096]{0,1:T(8,128)} fusion(bf16[4096,2176]{0,1:T(8,128)(2,1)} %reshape.67, bf16[256,2176]{1,0:T(8,128)(2,1)S(1)} %copy-done), kind=kOutput, calls=%fused_computation.10 | convolution fusion | flops 4563402752 | bytes 23134208 | tf_op jit(solution)/shard_map/dot_general | solution.py:35
  234.3 2.0 multiply_convert_fusion
  236.3 6.0 fusion.4
  242.2 26.2 %reshape.70 = bf16[32,64,34,64]{1,0,3,2:T(8,128)(2,1)} reshape(bf16[2048,2176]{0,1:T(8,128)(2,1)} %fusion.4) | data formatting | bytes 17825792 | tf_op jit(solution)/shard_map/reshape | solution.py:53
  268.5 24.4 %copy.33 = bf16[32,34,64,64]{3,2,1,0:T(8,128)(2,1)} copy(bf16[32,34,64,64]{2,0,3,1:T(8,128)(2,1)} %bitcast.26) | data formatting | bytes 17825792 | tf_op jit(solution)/shard_map/transpose | solution.py:53
  292.9 24.0 %reshape.71 = bf16[1088,4096]{1,0:T(8,128)(2,1)} reshape(bf16[32,34,64,64]{3,2,1,0:T(8,128)(2,1)} %copy.33) | data formatting | bytes 17825792 | tf_op jit(solution)/shard_map/reshape | solution.py:54
  316.9 6.0 fusion.6
  322.9 26.0 %reshape.68 = bf16[32,64,34,64]{1,0,3,2:T(8,128)(2,1)} reshape(bf16[2048,2176]{0,1:T(8,128)(2,1)} %fusion.6) | data formatting | bytes 17825792 | tf_op jit(solution)/shard_map/reshape | solution.py:53
  348.9 24.4 %copy.31 = bf16[32,34,64,64]{3,2,1,0:T(8,128)(2,1)} copy(bf16[32,34,64,64]{2,0,3,1:T(8,128)(2,1)} %bitcast.27) | data formatting | bytes 17825792 | tf_op jit(solution)/shard_map/transpose | solution.py:53
  373.3 24.0 %reshape.69 = bf16[1088,4096]{1,0:T(8,128)(2,1)} reshape(bf16[32,34,64,64]{3,2,1,0:T(8,128)(2,1)} %copy.31) | data formatting | bytes 17825792 | tf_op jit(solution)/shard_map/reshape | solution.py:54
  397.3 19.9 %gather_fusion.2 = bf16[896,4096]{1,0:T(8,128)(2,1)} fusion(bf16[1088,4096]{1,0:T(8,128)(2,1)} %reshape.71, s32[1024]{0:T(1024)S(1)} %get-tuple-element.23), kind=kCustom, calls=%fused_computation.1.clone | custom fusion | bytes 14683648 | tf_op jit(solution)/shard_map/jit(_take)/gather | solution.py:57
  417.2 19.7 %gather_fusion.1 = bf16[896,4096]{1,0:T(8,128)(2,1)} fusion(bf16[1088,4096]{1,0:T(8,128)(2,1)} %reshape.69, s32[1024]{0:T(1024)S(1)} %get-tuple-element.24), kind=kCustom, calls=%fused_computation.clone | custom fusion | bytes 14683648 | tf_op jit(solution)/shard_map/jit(_take)/gather | solution.py:57
  436.9 12.2 %fusion.1 = bf16[896,4096]{1,0:T(8,128)(2,1)} fusion(bf16[896,4096]{1,0:T(8,128)(2,1)} %gather_fusion.2, bf16[896,4096]{1,0:T(8,128)(2,1)} %gather_fusion.1, pred[896]{0:T(1024)(128)(4,1)S(1)} %get-tuple-element.19, pred[896]{0:T(1024)(128)(4,1)S(1)} %get-tuple-element.20, pred[896]{0:T(1024)(128)(4,1)S(1)} %get-tuple-element.18, pred[896]{0:T(1024)(128)(4,1)S(1)} %copy-done.2), kind=kLoop, calls=%fused_computation.6 | loop fusion | flops 14680064 | bytes 22023680 | tf_op jit(solution)/shard_map/convert_element_type | solution.py:61
  449.1 10.8 %copy.38 = bf16[896,4096]{0,1:T(8,128)(2,1)} copy(bf16[896,4096]{1,0:T(8,128)(2,1)} %fusion.1) | data formatting | bytes 14680064
  459.9 1.6 copy-done.1
  461.4 8.9 %fusion.3 = bf16[256,2176]{0,1:T(8,128)(2,1)S(1)} fusion(bf16[4096,2176]{0,1:T(8,128)(2,1)} %reshape.67, bf16[256,4096]{1,0:T(8,128)(2,1)S(1)} %copy-done.1), kind=kOutput, calls=%fused_computation.13 | convolution fusion | flops 4563959808 | bytes 21037056 | tf_op jit(solution)/shard_map/dot_general | solution.py:32
  470.4 1.5 copy.34
  471.9 1.1 convert_element_type.31
  473.0 0.8 copy.35
  473.8 216.2 %reduce-scatter.7.cloned.1.call-done = bf16[128,896]{1,0:T(8,128)(2,1)} async-done(((bf16[4096,896]{1,0:T(8,128)(2,1)}), bf16[128,896]{1,0:T(8,128)(2,1)}) %reduce-scatter.7.cloned.1.call-update) | async-done | bytes 229392
  690.0 1.1 copy.39
  691.1 0.8 convert_multiply_fusion
  (21 shorter events, 0.5 us)
Async XLA Ops:
  7.2 227.1 %all-gather.2.cloned.1.call-start = ((), (), s32[]{:S(2)}) async-start(), calls=%async_computation.2 | async-start | bytes 2359296 | tf_op jit(solution)/shard_map/all_gather | solution.py:10
  7.9 464.0 %reduce-scatter.5.cloned.1.call-start = ((), (), s32[]{:S(2)}) async-start(), calls=%async_computation.3 | async-start | bytes 4718592 | tf_op jit(solution)/shard_map/reduce_scatter | solution.py:38
  177.1 46.7 %copy-start = (bf16[256,2176]{1,0:T(8,128)(2,1)S(1)}, bf16[256,2176]{1,0:T(8,128)(2,1)}, u32[]{:S(2)}) copy-start(bf16[256,2176]{1,0:T(8,128)(2,1)} %param.8) | copy-start | bytes 3342340
  234.1 455.9 %reduce-scatter.7.cloned.1.call-start = ((), (), s32[]{:S(2)}) async-start(), calls=%async_computation.4 | async-start | bytes 7569408
  417.2 19.7 %copy-start.2 = (pred[896]{0:T(1024)(128)(4,1)S(1)}, pred[896]{0:T(1024)(128)(4,1)}, u32[]{:S(2)}) copy-start(pred[896]{0:T(1024)(128)(4,1)} %get-tuple-element.16) | copy-start | bytes 2692
  459.9 1.6 copy-start.1
Sparse Core Ops, SparseCore 0:
  9.8 29.6 all-gather.1
  234.2 39.6 reduce-scatter.4
  460.0 229.9 reduce-scatter.6
where the time goes:
time: 710 us; the launch traced here: 699 us
  local copies, waits for them, and re-layouts  393 us (55%)
  waiting for transfers between devices  217 us (31%)
  other arithmetic  43.4 us (6%)
  matrix products  31.2 us (4%)
  between operations  14.1 us (2%)
    unnamed x4, waiting for transfers between devices  217 us
    gather x3, local copies, waits for them, and re-layouts, body(): pair_blocks = jnp.take(padded_blocks, position, axis=0)  135 us
    reshape x2, local copies, waits for them, and re-layouts, body(): outer.reshape(half_rows, block_size, slot_count, block_size)  52.2 us
    transpose x2, local copies, waits for them, and re-layouts, body(): outer.reshape(half_rows, block_size, slot_count, block_size)  48.8 us
    reshape x2, local copies, waits for them, and re-layouts, body(): outer = outer.reshape(half_rows * slot_count, block_size * block_size)  48.1 us
    reshape x1, local copies, waits for them, and re-layouts, body(): dense_weight.transpose(0, 2, 1, 3)  46.7 us
    gather x2, local copies, waits for them, and re-layouts, body(): jnp.take(outer, jnp.clip(local_key, 0, half_rows * slot_count - 1), axis=0)  39.6 us
    transpose x1, other arithmetic, body(): dense_weight.transpose(0, 2, 1, 3)  24.1 us
  transfers between devices with their start and end apart: 3, of which 1 were waited for; matrix products, arithmetic and copies ran while one was open for 66% of the time, Pallas kernels for 0%

commit v1 on v0

v1 whole, which is shorter than its diff:
```python
import functools

import jax
import jax.numpy as jnp
from jax import lax
from jax.experimental import pallas as pl
from jax.experimental.pallas import tpu as pltpu
from jax.sharding import PartitionSpec as P

MESH = pl.DeviceIdType.MESH
BF = jnp.bfloat16
F32 = jnp.float32

NX, NZ, NY = 4, 8, 4
T = 256
F = 512
SLOTS = 34
PAIRS = 17
COLS = 2176
KEPT = 896
GROUPS = 56
HALF = KEPT // 2
REL_ORDER = (0, 1, 3, 2)


def dot(a, b):
    return jnp.dot(a, b, preferred_element_type=F32)


def dot_nt(a, b):
    return lax.dot_general(a, b, (((1,), (1,)), ((), ())), preferred_element_type=F32)


def square(v):
    w = v.astype(F32)
    return (w * w).astype(BF)


def kernel(
    tok, cot_hbm, wb_hbm, onehot, pick, slot_group, group_slot,
    hid, grads, curv,
    wb0, wb1, w, cotv, xf, xq, x2t, acc, gbuf, y, rp, rm, bp, bcore, by,
    loc_sem, xs, xr, a_s, ar, ts, tr, tcs, tcr, qs, qr, qcs, qcr, bcs, bcr, bys, byr, zps, zpr, zms, zmr,
):
    dp = lax.axis_index("dp")
    te = lax.axis_index("tensor")
    px = dp // NZ
    pz = lax.rem(dp, NZ)
    py = te // 2
    pc = lax.rem(te, 2)

    def at_x(d):
        return (lax.rem(px + d, NX) * NZ + pz, te)

    def at_z(d):
        return (px * NZ + lax.rem(pz + d, NZ), te)

    def at_y(d):
        return (dp, lax.rem(py + d, NY) * 2 + pc)

    other = (dp, py * 2 + (1 - pc))

    def send(src, dst, ssem, rsem, where):
        return pltpu.make_async_remote_copy(
            src_ref=src, dst_ref=dst, send_sem=ssem, recv_sem=rsem,
            device_id=where, device_id_type=MESH,
        )

    load_cot = pltpu.make_async_copy(cot_hbm, cotv.at[0], loc_sem.at[0])
    load_cot.start()

    def load_wb(kk, slot):
        return pltpu.make_async_copy(
            wb_hbm.at[:, :, pl.ds(pl.multiple_of(kk * 512, 512), 512)],
            (wb0, wb1)[slot].at[pl.ds(0, GROUPS)],
            loc_sem.at[1 + slot],
        )

    load_wb(0, 0).start()
    load_wb(1, 1).start()

    barrier = pltpu.get_barrier_semaphore()
    peers = [at_x(1), at_x(2), at_x(3), at_y(1), at_y(2), at_y(3), other, at_z(1), at_z(7)]
    for who in peers:
        pl.semaphore_signal(barrier, inc=1, device_id=who, device_id_type=MESH)

    fi = lax.broadcasted_iota(jnp.int32, (F, F), 0)
    ci = lax.broadcasted_iota(jnp.int32, (F, F), 1)
    perm = ((fi // 64 == ci % 8) & (fi % 64 == ci // 8)).astype(F32).astype(BF)
    xp = dot(tok[...], perm).astype(BF)
    for q in range(4):
        xf[te, q] = xp[:, q * 128 : (q + 1) * 128]
    wb0[GROUPS:, :, :] = jnp.zeros((4, 16, 512), BF)
    wb1[GROUPS:, :, :] = jnp.zeros((4, 16, 512), BF)

    pl.semaphore_wait(barrier, len(peers))

    a2a = []
    for d in (1, 2, 3):
        a2a.append(send(xf.at[te, lax.rem(px + d, NX)], xq.at[te, 3 - d], a_s.at[3 - d], ar.at[3 - d], at_x(d)))
    for c in a2a:
        c.start()
    tok_y = [send(xf.at[te], xf.at[te], ts.at[d - 1], tr.at[d - 1], at_y(d)) for d in (1, 2, 3)]
    for c in tok_y:
        c.start()
    tok_core = [send(xf.at[te], xf.at[te], tcs.at[0], tcr.at[0], other)]
    tok_core[0].start()

    load_cot.wait()
    top, bot = pl.ds(0, 128), pl.ds(128, 128)
    cx = [
        send(cotv.at[0, top], cotv.at[3, top], xs.at[0], xr.at[0], at_x(1)),
        send(cotv.at[0, bot], cotv.at[1, bot], xs.at[1], xr.at[1], at_x(3)),
        send(cotv.at[0, bot], cotv.at[3, bot], xs.at[2], xr.at[2], at_x(1)),
        send(cotv.at[0, top], cotv.at[1, top], xs.at[3], xr.at[3], at_x(3)),
    ]
    for c in cx:
        c.start()

    low = lax.broadcasted_iota(jnp.int32, (64, 128), 1) < 64

    def expand_group(q, ns, kk, slot):
        lhs = onehot[pl.ds(pl.multiple_of(q * 256, 128), ns * 64), pl.ds(0, ns * 64)]
        rhs = jnp.concatenate(
            [(wb0, wb1)[slot][pl.ds(slot_group[q * 4 + i], 4)].reshape(64, 512) for i in range(ns)], axis=0
        )
        out = dot(lhs, rhs)
        for k4 in range(4):
            for pair in range(ns // 2):
                a = out[pair * 128 : pair * 128 + 64, k4 * 128 : k4 * 128 + 128]
                b = out[pair * 128 + 64 : pair * 128 + 128, k4 * 128 : k4 * 128 + 128]
                p0 = jnp.where(low, a, pltpu.roll(b, 64, 1)).reshape(8, 1, 8, 128)
                p1 = jnp.where(low, pltpu.roll(a, 64, 1), b).reshape(8, 1, 8, 128)
                tile = jnp.concatenate([p0, p1], axis=1).reshape(8, 16, 128).astype(BF)
                w[:, kk * 4 + k4, :, pl.ds(pl.multiple_of(q * 256 + pair * 128, 128), 128)] = tile

    def expand_step(kk, slot):
        load_wb(kk, slot).wait()

        def group(q, carry):
            expand_group(q, 4, kk, slot)
            return carry

        lax.fori_loop(0, 8, group, 0)
        expand_group(8, 2, kk, slot)

    def expand_two(i, carry):
        for slot in range(2):
            expand_step(i * 2 + slot, slot)
            load_wb(i * 2 + 2 + slot, slot).start()
        return carry

    lax.fori_loop(0, 2, expand_two, 0)

    for c in a2a:
        c.wait_recv()
    xq_y = [send(xq.at[te], xq.at[te], qs.at[d - 1], qr.at[d - 1], at_y(d)) for d in (1, 2, 3)]
    for c in xq_y:
        c.start()
    xq_core = [send(xq.at[te], xq.at[te], qcs.at[0], qcr.at[0], other)]
    xq_core[0].start()

    lax.fori_loop(2, 3, expand_two, 0)
    for slot in range(2):
        expand_step(6 + slot, slot)

    def relay(buf, copies, core, ssem, rsem):
        for d in (1, 2, 3):
            copies[d - 1].wait_recv()
            src = lax.rem(py + NY - d, NY) * 2 + pc
            c = send(buf.at[src], buf.at[src], ssem.at[d], rsem.at[d], other)
            c.start()
            core.append(c)

    relay(xf, tok_y, tok_core, tcs, tcr)

    def back(j, carry):
        part = dot_nt(cotv[0], w[j].reshape(F, COLS))
        bp[lax.rem(j, 2) * 4 + j // 2] = part.astype(BF)
        return carry

    lax.fori_loop(0, 8, back, 0)
    b_core = send(bp.at[pl.ds((1 - pc) * 4, 4)], bcore, bcs.at[0], bcr.at[0], other)
    b_core.start()

    relay(xq, xq_y, xq_core, qcs, qcr)

    for c in tok_core:
        c.wait_recv()

    def hidden_tile(start, width):
        lhs = jnp.concatenate([xf[j, q] for j in range(8) for q in range(4)], axis=1)
        rhs = w[:, :, :, pl.ds(start, width)].reshape(4096, width)
        hid[:, pl.ds(start, width)] = dot(lhs, rhs).astype(BF)

    def hidden_step(n, carry):
        hidden_tile(pl.multiple_of(n * 256, 256), 256)
        return carry

    lax.fori_loop(0, 8, hidden_step, 0)
    hidden_tile(2048, 128)

    cx[0].wait_recv()
    fwd = [send(cotv.at[3, top], cotv.at[2, top], xs.at[4], xr.at[4], at_x(1))]
    fwd[0].start()
    cx[1].wait_recv()
    fwd.append(send(cotv.at[1, bot], cotv.at[2, bot], xs.at[5], xr.at[5], at_x(3)))
    fwd[1].start()

    b_core.wait_recv()
    b_y = []
    for d in (1, 2, 3):
        to = lax.rem(py + d, NY)
        total = bp[pc * 4 + to].astype(F32) + bcore[to].astype(F32)
        bp[pc * 4 + to] = total.astype(BF)
        c = send(bp.at[pc * 4 + to], by.at[d - 1], bys.at[d - 1], byr.at[d - 1], at_y(d))
        c.start()
        b_y.append(c)

    for c in xq_core:
        c.wait_recv()

    def put_square(j, rel, slab):
        at = REL_ORDER.index(rel)
        v = slab.astype(F32)
        v = (v * v).T.astype(BF)
        x2t[:, j, :, pl.ds(at * T, T)] = v.reshape(NZ, 16, T)

    def squares(j, carry):
        put_square(j, 0, xf[j, px])
        for d in (1, 2, 3):
            put_square(j, d, xq[j, d - 1])
        return carry

    lax.fori_loop(0, 8, squares, 0)

    cx[2].wait_recv()
    cx[3].wait_recv()

    def outer_tile(start, width):
        lhs = x2t[:, :, :, pl.ds(0, 3 * T)].reshape(1024, 3 * T)
        rhs = jnp.concatenate([square(cotv[r, :, pl.ds(start, width)]) for r in REL_ORDER[:3]], axis=0)
        acc[:, :, pl.ds(start, width)] = dot(lhs, rhs).reshape(NZ, 128, width)

    def outer_step(n, carry):
        outer_tile(pl.multiple_of(n * 256, 256), 256)
        return carry

    lax.fori_loop(0, 8, outer_step, 0)
    outer_tile(2048, 128)

    for c in fwd:
        c.wait_recv()

    def outer_last(start, width):
        lhs = x2t[:, :, :, pl.ds(3 * T, T)].reshape(1024, T)
        rhs = square(cotv[2, :, pl.ds(start, width)])
        acc[:, :, pl.ds(start, width)] += dot(lhs, rhs).reshape(NZ, 128, width)

    def outer_last_step(n, carry):
        outer_last(pl.multiple_of(n * 256, 256), 256)
        return carry

    lax.fori_loop(0, 8, outer_last_step, 0)
    outer_last(2048, 128)

    def chunks(da, db):
        for side, d in enumerate((da, db)):
            at = lax.rem(pz + d, NZ)

            def rearrange(pair, carry):
                o = acc[at, :, pl.ds(pl.multiple_of(pair * 128, 128), 128)].reshape(8, 2, 8, 128)
                p0 = o[:, 0].reshape(64, 128)
                p1 = o[:, 1].reshape(64, 128)
                a = jnp.where(low, p0, pltpu.roll(p1, 64, 1))
                b = jnp.where(low, pltpu.roll(p0, 64, 1), p1)
                gbuf[pair * 2, :, side * 128 : side * 128 + 128] = a.astype(BF)
                gbuf[pair * 2 + 1, :, side * 128 : side * 128 + 128] = b.astype(BF)
                return carry

            lax.fori_loop(0, PAIRS, rearrange, 0)

        def window(i, carry):
            rhs = jnp.concatenate([gbuf[group_slot[i * 4 + g]] for g in range(4)], axis=0)
            rows = pl.ds(pl.multiple_of(i * 64, 64), 64)
            out = dot(pick[rows, :], rhs).astype(BF)
            y[da, rows, :] = out[:, :128]
            y[db, rows, :] = out[:, 128:]
            return carry

        lax.fori_loop(0, 14, window, 0)

    rows_of = (pl.ds(0, HALF), pl.ds(HALF, HALF))

    def z_send(up, step, h):
        d = 4 - step if up else 4 + step
        buf, ssem, rsem, to = (rp, zps, zpr, at_z(1)) if up else (rm, zms, zmr, at_z(7))
        at = step * 2 + h
        return send(y.at[d, rows_of[h]], buf.at[step, rows_of[h]], ssem.at[at], rsem.at[at], to)

    sent = {}

    def z_step(up, step, h, add):
        if add:
            sent[(up, step - 1, h)].wait_recv()
            d = 4 - step if up else 4 + step
            buf = rp if up else rm
            y[d, rows_of[h], :] = (
                y[d, rows_of[h], :].astype(F32) + buf[step - 1, rows_of[h], :].astype(F32)
            ).astype(BF)
        c = z_send(up, step, h)
        c.start()
        sent[(up, step, h)] = c

    chunks(4, 3)
    z_step(True, 0, 0, False)
    z_step(False, 0, 1, False)
    z_step(True, 1, 1, False)
    chunks(5, 2)
    z_step(False, 1, 0, False)
    z_step(True, 1, 0, True)
    z_step(False, 1, 1, True)
    z_step(True, 2, 1, True)
    chunks(6, 1)
    z_step(False, 2, 0, True)
    chunks(7, 0)
    z_step(True, 2, 0, True)
    z_step(False, 2, 1, True)
    z_step(True, 3, 1, True)
    z_step(False, 3, 0, True)
    z_step(True, 3, 0, True)
    z_step(False, 3, 1, True)

    total = bp[pc * 4 + py].astype(F32) + bcore[py].astype(F32)
    for d in (1, 2, 3):
        b_y[d - 1].wait_recv()
        total = total + by[d - 1].astype(F32)
    grads[...] = dot_nt(total.astype(BF), perm).astype(BF)

    for h in range(2):
        sent[(True, 3, h)].wait_recv()
        sent[(False, 3, h)].wait_recv()
        value = (
            y[0, rows_of[h], :].astype(F32)
            + rp[3, rows_of[h], :].astype(F32)
            + rm[3, rows_of[h], :].astype(F32)
        )
        curv[rows_of[h], :] = value * (1.0 / 8192.0)

    for c in a2a + tok_y + tok_core + cx + xq_y + xq_core + fwd + [b_core] + b_y + list(sent.values()):
        c.wait_send()


def place_kernel(a, b, c, oa, ob, oc):
    oa[...] = a[...]
    ob[...] = b[...]
    oc[...] = c[...]


def tables(block_rows, block_slots):
    slot = jnp.arange(SLOTS * 64, dtype=jnp.int32)[:, None] // 64
    key = jnp.arange(SLOTS * 64, dtype=jnp.int32)[:, None]
    block = jnp.arange(KEPT, dtype=jnp.int32)[None, :]
    hit = (block_slots * 64 + block_rows)[None, :] == key
    before = (block_slots[None, :] < slot).astype(jnp.int32)
    offset = jnp.sum(jnp.where(hit, block + 65536, 0) - before, axis=1) - 65536
    lane = jnp.arange(256, dtype=jnp.int32)[None, :]
    here = (jnp.arange(SLOTS * 64, dtype=jnp.int32) // 64) % 4 * 64 + offset
    onehot = ((offset >= 0)[:, None] & (lane == here[:, None])).astype(BF)
    first = jnp.sum((block_slots[None, :] < jnp.arange(SLOTS, dtype=jnp.int32)[:, None]).astype(jnp.int32), axis=1)
    slot_group = first // 16
    place = (jnp.arange(KEPT, dtype=jnp.int32) // 16) % 4 * 64 + block_rows
    pick = (lane == place[:, None]).astype(BF)
    group_slot = block_slots[::16]
    return onehot, pick, slot_group, group_slot


def body(tokens, cotangent, weight_blocks, block_rows, block_slots):
    onehot, pick, slot_group, group_slot = tables(block_rows, block_slots)
    vm = pl.BlockSpec(memory_space=pltpu.VMEM)
    sm = pl.BlockSpec(memory_space=pltpu.SMEM)
    hb = pl.BlockSpec(memory_space=pl.ANY)
    sem = pltpu.SemaphoreType.DMA
    call = pl.pallas_call(
        kernel,
        out_shape=(
            jax.ShapeDtypeStruct((T, COLS), BF),
            jax.ShapeDtypeStruct((T, F), BF),
            jax.ShapeDtypeStruct((KEPT, 128), F32),
        ),
        in_specs=[vm, hb, hb, vm, vm, sm, sm],
        out_specs=(vm, vm, vm),
        scratch_shapes=[
            pltpu.VMEM((GROUPS + 4, 16, 512), BF),
            pltpu.VMEM((GROUPS + 4, 16, 512), BF),
            pltpu.VMEM((8, 32, 16, COLS), BF),
            pltpu.VMEM((4, T, COLS), BF),
            pltpu.VMEM((8, 4, T, 128), BF),
            pltpu.VMEM((8, 3, T, 128), BF),
            pltpu.VMEM((NZ, 8, 16, 4 * T), BF),
            pltpu.VMEM((NZ, 128, COLS), F32),
            pltpu.VMEM((SLOTS, 64, 256), BF),
            pltpu.VMEM((8, KEPT, 128), BF),
            pltpu.VMEM((4, KEPT, 128), BF),
            pltpu.VMEM((4, KEPT, 128), BF),
            pltpu.VMEM((8, T, F), BF),
            pltpu.VMEM((4, T, F), BF),
            pltpu.VMEM((3, T, F), BF),
            sem((3,)),
            sem((6,)), sem((6,)),
            sem((3,)), sem((3,)),
            sem((3,)), sem((3,)),
            sem((4,)), sem((4,)),
            sem((3,)), sem((3,)),
            sem((4,)), sem((4,)),
            sem((1,)), sem((1,)),
            sem((3,)), sem((3,)),
            sem((8,)), sem((8,)),
            sem((8,)), sem((8,)),
        ],
        compiler_params=pltpu.CompilerParams(
            collective_id=0, has_side_effects=True, vmem_limit_bytes=62 * 2**20
        ),
        cost_estimate=pl.CostEstimate(flops=14_000_000_000, bytes_accessed=12_000_000, transcendentals=0),
    )
    outs = call(tokens, cotangent, weight_blocks.reshape(GROUPS, 16, 4096), onehot, pick, slot_group, group_slot)
    place = pl.pallas_call(
        place_kernel,
        out_shape=[jax.ShapeDtypeStruct(o.shape, o.dtype) for o in outs],
        in_specs=[vm] * 3,
        out_specs=[vm] * 3,
    )
    return tuple(place(*outs))


def solution(mesh):
    placed = (P("dp", "tensor"), P("dp", "tensor"), P("tensor", None), P("tensor"), P("tensor"))
    return jax.shard_map(
        body,
        mesh=mesh,
        in_specs=placed,
        out_specs=(P("dp", "tensor"), P("dp", "tensor"), P("tensor", "dp")),
        check_vma=False,
    )
```

time: 710 us -> 107 us (0.15); the launches traced: 699 us -> 106 us
  local copies, waits for them, and re-layouts: 393 us -> 1.34 us
  waiting for transfers between devices: 217 us -> 0 us
  Pallas kernels: 0 us -> 96.1 us
  other arithmetic: 43.4 us -> 8.12 us
  matrix products: 31.2 us -> 0 us
  between operations: 14.1 us -> 0.65 us
    unnamed x4 -> x0, waiting for transfers between devices: 217 us -> none
    gather x5 -> x0, local copies, waits for them, and re-layouts: 174 us -> none  [the longest x3 135 us: body(): pair_blocks = jnp.take(padded_blocks, position, axis=0)]
    reshape x5 -> x0, local copies, waits for them, and re-layouts: 147 us -> none  [the longest x2 52.2 us: body(): outer.reshape(half_rows, block_size, slot_count, block_size)]
    pallas_call x0 -> x2, Pallas kernels: none -> 96.1 us  [the longest x1 93.4 us: body(): call(tokens, cotangent, weight_blocks.reshape(GROUPS, 16, 4096), onehot,...]
    transpose x2 -> x0, local copies, waits for them, and re-layouts: 48.8 us -> none  [body(): outer.reshape(half_rows, block_size, slot_count, block_size)]
    dot_general x4 -> x0, matrix products: 31.2 us -> none  [the longest x2 12 us: body(): lax.dot_general(square_part, squared_back, (((0,), (0,)), ((), ())), pref...]
    transpose x1 -> x0, other arithmetic: 24.1 us -> none  [body(): dense_weight.transpose(0, 2, 1, 3)]
    unnamed x10 -> x0, local copies, waits for them, and re-layouts: 15.8 us -> none
  transfers between devices with their start and end apart: 3 -> 0, of which waited for: 1 -> 0; matrix products, arithmetic and copies ran while one was open for 66% -> 0% of each run, Pallas kernels for 0% -> 0%
where the time goes in v1:
time: 107 us; the launch traced here: 106 us
  Pallas kernels  96.1 us (90%)
  other arithmetic  8.12 us (8%)
  local copies, waits for them, and re-layouts  1.34 us (1%)
    pallas_call x1, Pallas kernels, body(): call(tokens, cotangent, weight_blocks.reshape(GROUPS, 16, 4096), onehot,...  93.4 us
    pallas_call x1, Pallas kernels, body(): return tuple(place(*outs))  2.67 us
    reduce_sum x1, other arithmetic, tables(): offset = jnp.sum(jnp.where(hit, block + 65536, 0) - before, axis=1) - 65536  2.63 us
    convert_element_type x1, other arithmetic, tables(): onehot = ((offset >= 0)[:, None] & (lane == here[:, None])).astype(BF)  2.46 us

profile of v1, /device:TPU:8, one launch (start us, length us, event | category | flops | bytes accessed | tf_op | source)
XLA Modules:
  0.0 106.2 jit_solution(17400193145885199060)
XLA Ops:
  0.6 1.3 %slice.3.group_slot = s32[56]{0:T(128)} slice(s32[896]{0:T(1024)} %param.9), slice={[0:896:16]} | slice | bytes 448 | tf_op jit(solution)/shard_map/slice | solution.py:374
  2.0 0.8 convert_reduce_fusion
  2.8 0.5 and_select_fusion.slot_group
  3.3 0.7 fusion.11
  4.0 2.6 %subtract_reduce_fusion = s32[2176]{0:T(1024)S(1)} fusion(s32[896]{0:T(1024)} %param.9, s32[896]{0:T(1024)S(1)} %get-tuple-element.11, s32[896]{0:T(1024)S(1)} %get-tuple-element.10, s32[2176]{0:T(1024)S(1)} %add_select_fusion.1), kind=kLoop, calls=%fused_computation | loop fusion | flops 11696000 | bytes 28160 | tf_op jit(solution)/shard_map/reduce_sum | solution.py:366
  6.7 1.0 fusion.2.pick
  7.6 2.5 %fusion.1.onehot = bf16[2176,256]{1,0:T(8,128)(2,1)} fusion(s32[2176]{0:T(1024)S(1)} %fusion.5, pred[2176]{0:T(1024)(128)(4,1)S(1)} %add_compare_fusion), kind=kLoop, calls=%fused_computation.4 | loop fusion | flops 1671168 | bytes 1124992 | tf_op jit(solution)/shard_map/convert_element_type | solution.py:369
  10.1 93.4 %shard_map.76 = (bf16[256,2176]{1,0:T(8,128)(2,1)}, bf16[256,512]{1,0:T(8,128)(2,1)}, f32[896,128]{1,0:T(8,128)}) custom-call(bf16[256,512]{1,0:T(8,128)(2,1)} %tok.1, bf16[256,2176]{1,0:T(8,128)(2,1)} %cot_hbm.1, bf16[56,16,4096]{2,1,0:T(8,128)(2,1)} %bitcast.1, bf16[2176,256]{1,0:T(8,128)(2,1)} %fusion.1.onehot, bf16[896,256]{1,0:T(8,128)(2,1)} %fusion.2.pick, ...), custom_call_target="tpu_custom_call" | custom-call | flops 14000000000 | bytes 12000000 | tf_op jit(solution)/shard_map/pallas_call | solution.py:426
  103.6 2.7 %shard_map.77 = (bf16[256,2176]{1,0:T(8,128)(2,1)}, bf16[256,512]{1,0:T(8,128)(2,1)}, f32[896,128]{1,0:T(8,128)}) custom-call(bf16[256,2176]{1,0:T(8,128)(2,1)} %get-tuple-element.6.a, bf16[256,512]{1,0:T(8,128)(2,1)} %get-tuple-element.7.b, f32[896,128]{1,0:T(8,128)} %get-tuple-element.8.c), custom_call_target="tpu_custom_call" | custom-call | tf_op jit(solution)/shard_map/pallas_call | solution.py:433
  (3 shorter events, 0.0 us)

commit v2 on v1

v2 whole, which is shorter than its diff:
```python
import functools

import jax
import jax.numpy as jnp
from jax import lax
from jax.experimental import pallas as pl
from jax.experimental.pallas import tpu as pltpu
from jax.sharding import PartitionSpec as P

MESH = pl.DeviceIdType.MESH
BF = jnp.bfloat16
F32 = jnp.float32

NX, NZ, NY = 4, 8, 4
T = 256
F = 512
SLOTS = 34
PAIRS = 17
COLS = 2176
KEPT = 896
GROUPS = 56
QUARTER = KEPT // 4
REL_ORDER = (0, 1, 3, 2)


def dot(a, b):
    return jnp.dot(a, b, preferred_element_type=F32)


def dot_nt(a, b):
    return lax.dot_general(a, b, (((1,), (1,)), ((), ())), preferred_element_type=F32)


def square(v):
    w = v.astype(F32)
    return (w * w).astype(BF)


def kernel(
    tok, cot_hbm, wb_hbm, windows, slots,
    hid, grads, curv,
    slot_first, pick, onehot, wb0, wb1, w, cotv, xf, xq, x2t, acc, gbuf, y, rp, rm, bp, bcore, by,
    loc_sem, xs, xr, a_s, ar, ts, tr, tcs, tcr, qs, qr, qcs, qcr, bcs, bcr, bys, byr, zps, zpr, zms, zmr,
):
    dp = lax.axis_index("dp")
    te = lax.axis_index("tensor")
    px = dp // NZ
    pz = lax.rem(dp, NZ)
    py = te // 2
    pc = lax.rem(te, 2)

    def at_x(d):
        return (lax.rem(px + d, NX) * NZ + pz, te)

    def at_z(d):
        return (px * NZ + lax.rem(pz + d, NZ), te)

    def at_y(d):
        return (dp, lax.rem(py + d, NY) * 2 + pc)

    other = (dp, py * 2 + (1 - pc))

    def send(src, dst, ssem, rsem, where):
        return pltpu.make_async_remote_copy(
            src_ref=src, dst_ref=dst, send_sem=ssem, recv_sem=rsem,
            device_id=where, device_id_type=MESH,
        )

    load_cot = pltpu.make_async_copy(cot_hbm, cotv.at[0], loc_sem.at[0])
    load_cot.start()

    def load_wb(kk, slot):
        return pltpu.make_async_copy(
            wb_hbm.at[:, :, pl.ds(pl.multiple_of(kk * 512, 512), 512)],
            (wb0, wb1)[slot].at[pl.ds(0, GROUPS)],
            loc_sem.at[1 + slot],
        )

    load_wb(0, 0).start()
    load_wb(1, 1).start()

    barrier = pltpu.get_barrier_semaphore()
    peers = [at_x(1), at_x(2), at_x(3), at_y(1), at_y(2), at_y(3), other, at_z(1), at_z(7)]
    for who in peers:
        pl.semaphore_signal(barrier, inc=1, device_id=who, device_id_type=MESH)

    fi = lax.broadcasted_iota(jnp.int32, (F, F), 0)
    ci = lax.broadcasted_iota(jnp.int32, (F, F), 1)
    perm = ((fi // 64 == ci % 8) & (fi % 64 == ci // 8)).astype(F32).astype(BF)
    xp = dot(tok[...], perm).astype(BF)
    for q in range(4):
        xf[te, q] = xp[:, q * 128 : (q + 1) * 128]
    wb0[GROUPS:, :, :] = jnp.zeros((4, 16, 512), BF)
    wb1[GROUPS:, :, :] = jnp.zeros((4, 16, 512), BF)

    lane = lax.broadcasted_iota(jnp.int32, (1, 128), 1)

    def slot_step(s, at):
        slot_first[s] = at
        here = slots[jnp.minimum(at, GROUPS - 1) * 16]
        there = slots[jnp.minimum(at + 1, GROUPS - 1) * 16]
        one = (at < GROUPS) & (here == s)
        three = (at + 1 < GROUPS) & (there == s)
        return at + jnp.where(one, jnp.where(three, 3, 1), 0)

    lax.fori_loop(0, SLOTS, slot_step, jnp.int32(0))

    def pick_step(v, carry):
        k = jnp.where(lane < 64, windows[pl.ds(v * 8, 1), :], windows[pl.ds(v * 8 + 4, 1), :])
        wanted = lax.rem(lane, 64) // 16 * 64 + lax.rem(k, 64)
        e = (lax.broadcasted_iota(jnp.int32, (256, 128), 0) == wanted).astype(F32)
        pick[pl.ds(pl.multiple_of(v * 128, 128), 128), :] = e.T.astype(BF)
        return carry

    def place_rows(q, ns):
        parts = []
        for i in range(0, ns, 2):
            s = q * 4 + i
            k0 = windows[pl.ds(slot_first[s], 1), :] - s * 64
            k1 = windows[pl.ds(slot_first[s + 1], 1), :] - (s * 64 + 64)
            k = jnp.where(lane < 64, k0, k1)
            base = jnp.where(lane < 64, i * 64, i * 64 + 64)
            parts.append(jnp.where((k >= 0) & (k < 64), k + base, -1))
        wanted = jnp.concatenate(parts, axis=1) if len(parts) > 1 else parts[0]
        n = ns * 64
        e = (lax.broadcasted_iota(jnp.int32, (n, n), 0) == wanted).astype(F32).astype(BF)
        onehot[pl.ds(pl.multiple_of(q * 256, 256), n), pl.ds(0, n)] = e

    def place_step(q, carry):
        place_rows(q, 4)
        return carry

    lax.fori_loop(0, 8, place_step, 0)
    place_rows(8, 2)

    pl.semaphore_wait(barrier, len(peers))

    a2a = []
    for d in (1, 2, 3):
        a2a.append(send(xf.at[te, lax.rem(px + d, NX)], xq.at[te, 3 - d], a_s.at[3 - d], ar.at[3 - d], at_x(d)))
    for c in a2a:
        c.start()
    tok_y = [send(xf.at[te], xf.at[te], ts.at[d - 1], tr.at[d - 1], at_y(d)) for d in (1, 2, 3)]
    for c in tok_y:
        c.start()
    tok_core = [send(xf.at[te], xf.at[te], tcs.at[0], tcr.at[0], other)]
    tok_core[0].start()

    load_cot.wait()
    parts = [pl.ds(i * 64, 64) for i in range(4)]
    cx = []

    def send_part(i):
        at = len(cx)
        cx.append(send(cotv.at[0, parts[i]], cotv.at[3, parts[i]], xs.at[at], xr.at[at], at_x(1)))
        cx[-1].start()
        at += 1
        cx.append(send(cotv.at[0, parts[3 - i]], cotv.at[1, parts[3 - i]], xs.at[at], xr.at[at], at_x(3)))
        cx[-1].start()

    send_part(0)
    send_part(1)

    low = lax.broadcasted_iota(jnp.int32, (64, 128), 1) < 64

    def expand_group(q, ns, kk, slot):
        lhs = onehot[pl.ds(pl.multiple_of(q * 256, 256), ns * 64), pl.ds(0, ns * 64)]
        buf = (wb0, wb1)[slot]
        firsts = [slot_first[q * 4 + i] for i in range(ns)]
        for side in range(2):
            rhs = jnp.concatenate(
                [buf[pl.ds(first, 4), :, pl.ds(side * 256, 256)].reshape(64, 256) for first in firsts], axis=0
            )
            out = dot(lhs, rhs)
            for pair in range(ns // 2):
                for k2 in range(2):
                    a = out[pair * 128 : pair * 128 + 64, k2 * 128 : k2 * 128 + 128]
                    b = out[pair * 128 + 64 : pair * 128 + 128, k2 * 128 : k2 * 128 + 128]
                    p0 = jnp.where(low, a, pltpu.roll(b, 64, 1)).reshape(8, 1, 8, 128)
                    p1 = jnp.where(low, pltpu.roll(a, 64, 1), b).reshape(8, 1, 8, 128)
                    tile = jnp.concatenate([p0, p1], axis=1).reshape(8, 16, 128).astype(BF)
                    w[:, kk * 4 + side * 2 + k2, :, pl.ds(pl.multiple_of(q * 256 + pair * 128, 128), 128)] = tile

    def expand_step(kk, slot):
        load_wb(kk, slot).wait()

        def group(q, carry):
            expand_group(q, 4, kk, slot)
            return carry

        lax.fori_loop(0, 8, group, 0, unroll=2)
        expand_group(8, 2, kk, slot)

    def expand_two(i, carry):
        for slot in range(2):
            expand_step(i * 2 + slot, slot)
            load_wb(i * 2 + 2 + slot, slot).start()
        return carry

    lax.fori_loop(0, 2, expand_two, 0)

    cx[0].wait_send()
    cx[1].wait_send()
    send_part(2)

    for c in a2a:
        c.wait_recv()
    xq_y = [send(xq.at[te], xq.at[te], qs.at[d - 1], qr.at[d - 1], at_y(d)) for d in (1, 2, 3)]
    for c in xq_y:
        c.start()
    xq_core = [send(xq.at[te], xq.at[te], qcs.at[0], qcr.at[0], other)]
    xq_core[0].start()

    lax.fori_loop(2, 3, expand_two, 0)
    for slot in range(2):
        expand_step(6 + slot, slot)

    def relay(buf, copies, core, ssem, rsem):
        for d in (1, 2, 3):
            copies[d - 1].wait_recv()
            src = lax.rem(py + NY - d, NY) * 2 + pc
            c = send(buf.at[src], buf.at[src], ssem.at[d], rsem.at[d], other)
            c.start()
            core.append(c)

    cx[2].wait_send()
    cx[3].wait_send()
    send_part(3)

    relay(xf, tok_y, tok_core, tcs, tcr)

    def back(j, carry):
        part = dot_nt(w[pl.ds(j * 2, 2)].reshape(2 * F, COLS), cotv[0]).astype(BF)
        bp[j] = part[:F]
        bp[4 + j] = part[F:]
        return carry

    lax.fori_loop(0, 4, back, 0)
    b_core = send(bp.at[pl.ds((1 - pc) * 4, 4)], bcore, bcs.at[0], bcr.at[0], other)
    b_core.start()

    fwd = []
    for i in (0, 1):
        cx[2 * i].wait_recv()
        fwd.append(send(cotv.at[3, parts[i]], cotv.at[2, parts[i]], xs.at[8 + 2 * i], xr.at[8 + 2 * i], at_x(1)))
        fwd[-1].start()
        cx[2 * i + 1].wait_recv()
        fwd.append(
            send(cotv.at[1, parts[3 - i]], cotv.at[2, parts[3 - i]], xs.at[9 + 2 * i], xr.at[9 + 2 * i], at_x(3))
        )
        fwd[-1].start()

    relay(xq, xq_y, xq_core, qcs, qcr)

    for c in tok_core:
        c.wait_recv()

    def hidden_tile(start, width):
        lhs = jnp.concatenate([xf[j, q] for j in range(8) for q in range(4)], axis=1)
        rhs = w[:, :, :, pl.ds(start, width)].reshape(4096, width)
        hid[:, pl.ds(start, width)] = dot(lhs, rhs).astype(BF)

    def hidden_step(n, carry):
        hidden_tile(pl.multiple_of(n * 256, 256), 256)
        return carry

    lax.fori_loop(0, 8, hidden_step, 0)
    lax.fori_loop(0, 7, pick_step, 0)
    hidden_tile(2048, 128)

    b_core.wait_recv()
    b_y = []
    for d in (1, 2, 3):
        to = lax.rem(py + d, NY)
        total = bp[pc * 4 + to].astype(F32) + bcore[to].astype(F32)
        bp[pc * 4 + to] = total.astype(BF)
        c = send(bp.at[pc * 4 + to], by.at[d - 1], bys.at[d - 1], byr.at[d - 1], at_y(d))
        c.start()
        b_y.append(c)

    for c in xq_core:
        c.wait_recv()

    def put_square(j, rel, slab):
        at = REL_ORDER.index(rel)
        v = slab.astype(F32)
        v = (v * v).T.astype(BF)
        x2t[:, j, :, pl.ds(at * T, T)] = v.reshape(NZ, 16, T)

    def squares(j, carry):
        put_square(j, 0, xf[j, px])
        for d in (1, 2, 3):
            put_square(j, d, xq[j, d - 1])
        return carry

    lax.fori_loop(0, 8, squares, 0)

    for c in cx[4:]:
        c.wait_recv()

    def outer_tile(start, width):
        lhs = x2t[:, :, :, pl.ds(0, 3 * T)].reshape(1024, 3 * T)
        rhs = jnp.concatenate([square(cotv[r, :, pl.ds(start, width)]) for r in REL_ORDER[:3]], axis=0)
        acc[:, :, pl.ds(start, width)] = dot(lhs, rhs).reshape(NZ, 128, width)

    def outer_step(n, carry):
        outer_tile(pl.multiple_of(n * 256, 256), 256)
        return carry

    lax.fori_loop(0, 8, outer_step, 0)
    outer_tile(2048, 128)

    for c in fwd:
        c.wait_recv()

    def square_last(i, carry):
        rows = pl.ds(pl.multiple_of(i * 64, 64), 64)
        cotv[2, rows, :] = square(cotv[2, rows, :])
        return carry

    lax.fori_loop(0, 4, square_last, 0)

    def chunks(da, db):
        at = [lax.rem(pz + d, NZ) for d in (da, db)]

        def rearrange(start, width):
            lhs = jnp.concatenate([x2t[z, :, :, pl.ds(3 * T, T)].reshape(128, T) for z in at], axis=0)
            last = dot(lhs, cotv[2, :, pl.ds(start, width)])
            for side in range(2):
                whole = acc[at[side], :, pl.ds(start, width)] + last[side * 128 : side * 128 + 128]
                for pair in range(width // 128):
                    o = whole[:, pair * 128 : pair * 128 + 128].reshape(8, 2, 8, 128)
                    p0 = o[:, 0].reshape(64, 128)
                    p1 = o[:, 1].reshape(64, 128)
                    a = jnp.where(low, p0, pltpu.roll(p1, 64, 1))
                    b = jnp.where(low, pltpu.roll(p0, 64, 1), p1)
                    slot = start // 64 + pair * 2
                    gbuf[slot, :, side * 128 : side * 128 + 128] = a.astype(BF)
                    gbuf[slot + 1, :, side * 128 : side * 128 + 128] = b.astype(BF)

        def rearrange_step(n, carry):
            rearrange(pl.multiple_of(n * 256, 256), 256)
            return carry

        lax.fori_loop(0, 8, rearrange_step, 0, unroll=2)
        rearrange(2048, 128)

        def window(i, carry):
            rhs = jnp.concatenate([gbuf[slots[(i * 4 + g) * 16]] for g in range(4)], axis=0)
            rows = pl.ds(pl.multiple_of(i * 64, 64), 64)
            out = dot(pick[rows, :], rhs).astype(BF)
            y[da, rows, :] = out[:, :128]
            y[db, rows, :] = out[:, 128:]
            return carry

        lax.fori_loop(0, 14, window, 0, unroll=7)

    rows_of = [pl.ds(i * QUARTER, QUARTER) for i in range(4)]
    sent = {}

    def z_step(up, step, h):
        d = 4 - step if up else 4 + step
        buf, ssem, rsem, to = (rp, zps, zpr, at_z(1)) if up else (rm, zms, zmr, at_z(7))
        rows = rows_of[h]
        if (up, step - 1, h) in sent:
            sent[(up, step - 1, h)].wait_recv()
            y[d, rows, :] = (y[d, rows, :].astype(F32) + buf[step - 1, rows, :].astype(F32)).astype(BF)
        at = step * 4 + h
        c = send(y.at[d, rows], buf.at[step, rows], ssem.at[at], rsem.at[at], to)
        c.start()
        sent[(up, step, h)] = c

    def z_steps(up, step, parts_of):
        for h in parts_of:
            z_step(up, step, h)

    chunks(4, 3)
    z_steps(True, 0, (0, 1))
    z_steps(False, 0, (3, 2))
    z_steps(True, 1, (2, 3))
    chunks(5, 2)
    z_steps(False, 1, (1, 0))
    z_steps(True, 1, (0, 1))
    z_steps(False, 1, (3, 2))
    chunks(6, 1)
    z_steps(True, 2, (2, 3))
    z_steps(False, 2, (1, 0))
    z_steps(True, 2, (0, 1))
    z_steps(False, 2, (3, 2))
    chunks(7, 0)
    z_steps(True, 3, (2, 3))
    z_steps(False, 3, (1, 0))
    z_steps(True, 3, (0, 1))
    z_steps(False, 3, (3, 2))

    total = bp[pc * 4 + py].astype(F32) + bcore[py].astype(F32)
    for d in (1, 2, 3):
        b_y[d - 1].wait_recv()
        total = total + by[d - 1].astype(F32)
    grads[...] = dot(perm, total.astype(BF)).T.astype(BF)

    for h in (2, 1, 0, 3):
        sent[(True, 3, h)].wait_recv()
        sent[(False, 3, h)].wait_recv()
        value = (
            y[0, rows_of[h], :].astype(F32)
            + rp[3, rows_of[h], :].astype(F32)
            + rm[3, rows_of[h], :].astype(F32)
        )
        curv[rows_of[h], :] = value * (1.0 / 8192.0)

    for c in a2a + tok_y + tok_core + cx[4:] + xq_y + xq_core + fwd + [b_core] + b_y + list(sent.values()):
        c.wait_send()


def place_kernel(a, b, c, oa, ob, oc):
    oa[...] = a[...]
    ob[...] = b[...]
    oc[...] = c[...]


def tables(block_rows, block_slots):
    keys = jnp.pad(block_slots * 64 + block_rows, (0, 128), constant_values=-1).reshape(64, 16)
    window = jnp.concatenate([keys[i : i + 60] for i in range(4)] * 2, axis=1)
    return window


def body(tokens, cotangent, weight_blocks, block_rows, block_slots):
    window = tables(block_rows, block_slots)
    vm = pl.BlockSpec(memory_space=pltpu.VMEM)
    sm = pl.BlockSpec(memory_space=pltpu.SMEM)
    hb = pl.BlockSpec(memory_space=pl.ANY)
    sem = pltpu.SemaphoreType.DMA
    call = pl.pallas_call(
        kernel,
        out_shape=(
            jax.ShapeDtypeStruct((T, COLS), BF),
            jax.ShapeDtypeStruct((T, F), BF),
            jax.ShapeDtypeStruct((KEPT, 128), F32),
        ),
        in_specs=[vm, hb, hb, vm, sm],
        out_specs=(vm, vm, vm),
        scratch_shapes=[
            pltpu.SMEM((SLOTS,), jnp.int32),
            pltpu.VMEM((KEPT, 256), BF),
            pltpu.VMEM((SLOTS * 64, 256), BF),
            pltpu.VMEM((GROUPS + 4, 16, 512), BF),
            pltpu.VMEM((GROUPS + 4, 16, 512), BF),
            pltpu.VMEM((8, 32, 16, COLS), BF),
            pltpu.VMEM((4, T, COLS), BF),
            pltpu.VMEM((8, 4, T, 128), BF),
            pltpu.VMEM((8, 3, T, 128), BF),
            pltpu.VMEM((NZ, 8, 16, 4 * T), BF),
            pltpu.VMEM((NZ, 128, COLS), F32),
            pltpu.VMEM((SLOTS, 64, 256), BF),
            pltpu.VMEM((8, KEPT, 128), BF),
            pltpu.VMEM((4, KEPT, 128), BF),
            pltpu.VMEM((4, KEPT, 128), BF),
            pltpu.VMEM((8, F, T), BF),
            pltpu.VMEM((4, F, T), BF),
            pltpu.VMEM((3, F, T), BF),
            sem((3,)),
            sem((12,)), sem((12,)),
            sem((3,)), sem((3,)),
            sem((3,)), sem((3,)),
            sem((4,)), sem((4,)),
            sem((3,)), sem((3,)),
            sem((4,)), sem((4,)),
            sem((1,)), sem((1,)),
            sem((3,)), sem((3,)),
            sem((16,)), sem((16,)),
            sem((16,)), sem((16,)),
        ],
        compiler_params=pltpu.CompilerParams(
            collective_id=0, has_side_effects=True, vmem_limit_bytes=62 * 2**20
        ),
        cost_estimate=pl.CostEstimate(flops=14_000_000_000, bytes_accessed=12_000_000, transcendentals=0),
    )
    outs = call(tokens, cotangent, weight_blocks.reshape(GROUPS, 16, 4096), window, block_slots)
    place = pl.pallas_call(
        place_kernel,
        out_shape=[jax.ShapeDtypeStruct(o.shape, o.dtype) for o in outs],
        in_specs=[vm] * 3,
        out_specs=[vm] * 3,
    )
    return tuple(place(*outs))


def solution(mesh):
    placed = (P("dp", "tensor"), P("dp", "tensor"), P("tensor", None), P("tensor"), P("tensor"))
    return jax.shard_map(
        body,
        mesh=mesh,
        in_specs=placed,
        out_specs=(P("dp", "tensor"), P("dp", "tensor"), P("tensor", "dp")),
        check_vma=False,
    )
```

time: 107 us -> 78.4 us (0.73)
  Pallas kernels: 96.1 us -> 75.7 us
  other arithmetic: 8.12 us -> 0.71 us
    pallas_call x1, Pallas kernels: 93.4 us -> 73 us  [body(): call(tokens, cotangent, weight_blocks.reshape(GROUPS, 16, 4096), window,...]
    reduce_sum x2 -> x0, other arithmetic: 3.44 us -> none  [the longest x1 2.63 us: tables(): offset = jnp.sum(jnp.where(hit, block + 65536, 0) - before, axis=1) - 65536]
    convert_element_type x2 -> x0, other arithmetic: 3.42 us -> none  [the longest x1 2.46 us: tables(): onehot = ((offset >= 0)[:, None] & (lane == here[:, None])).astype(BF)]
where the time goes in v2:
time: 78.4 us; the launch traced here: 78.2 us
  Pallas kernels  75.7 us (97%)
  local copies, waits for them, and re-layouts  1.12 us (1%)
    pallas_call x1, Pallas kernels, body(): call(tokens, cotangent, weight_blocks.reshape(GROUPS, 16, 4096), window,...  73 us
    pallas_call x1, Pallas kernels, body(): return tuple(place(*outs))  2.67 us

profile of v2, /device:TPU:8, one launch (start us, length us, event | category | flops | bytes accessed | tf_op | source)
XLA Modules:
  0.0 78.2 jit_solution(9901941295919386669)
XLA Ops:
  0.6 0.7 multiply_add_fusion
  1.3 0.1 pad_slice_fusion
  1.4 0.1 slice.63
  1.5 0.1 slice.59
  1.6 0.1 slice.61
  1.6 0.1 slice.57
  1.7 0.8 concatenate.3.windows
  2.5 73.0 %shard_map.76 = (bf16[256,2176]{1,0:T(8,128)(2,1)}, bf16[256,512]{1,0:T(8,128)(2,1)}, f32[896,128]{1,0:T(8,128)}) custom-call(bf16[256,512]{1,0:T(8,128)(2,1)} %tok.1, bf16[256,2176]{1,0:T(8,128)(2,1)} %cot_hbm.1, bf16[56,16,4096]{2,1,0:T(8,128)(2,1)} %bitcast.1, s32[60,128]{1,0:T(8,128)} %concatenate.3.windows, s32[896]{0:T(1024)} %slots.1), custom_call_target="tpu_custom_call" | custom-call | flops 14000000000 | bytes 12000000 | tf_op jit(solution)/shard_map/pallas_call | solution.py:479
  75.5 2.7 %shard_map.77 = (bf16[256,2176]{1,0:T(8,128)(2,1)}, bf16[256,512]{1,0:T(8,128)(2,1)}, f32[896,128]{1,0:T(8,128)}) custom-call(bf16[256,2176]{1,0:T(8,128)(2,1)} %get-tuple-element.6.a, bf16[256,512]{1,0:T(8,128)(2,1)} %get-tuple-element.7.b, f32[896,128]{1,0:T(8,128)} %get-tuple-element.8.c), custom_call_target="tpu_custom_call" | custom-call | tf_op jit(solution)/shard_map/pallas_call | solution.py:486

commit v3 on v2

--- a/solution.py
+++ b/solution.py
@@ -20,6 +20,7 @@
 KEPT = 896
 GROUPS = 56
 QUARTER = KEPT // 4
+EARLY = 1664
 REL_ORDER = (0, 1, 3, 2)
 
 
@@ -38,8 +39,8 @@
 
 def kernel(
     tok, cot_hbm, wb_hbm, windows, slots,
-    hid, grads, curv,
-    slot_first, pick, onehot, wb0, wb1, w, cotv, xf, xq, x2t, acc, gbuf, y, rp, rm, bp, bcore, by,
+    hid_out, grads_out, curv,
+    hid, grads, slot_first, pick, onehot, wb0, wb1, w, cotv, xf, xq, x2t, acc, gbuf, y, rp, rm, bp, bcore, by,
     loc_sem, xs, xr, a_s, ar, ts, tr, tcs, tcr, qs, qr, qcs, qcr, bcs, bcr, bys, byr, zps, zpr, zms, zmr,
 ):
     dp = lax.axis_index("dp")
@@ -92,6 +93,34 @@
         xf[te, q] = xp[:, q * 128 : (q + 1) * 128]
     wb0[GROUPS:, :, :] = jnp.zeros((4, 16, 512), BF)
     wb1[GROUPS:, :, :] = jnp.zeros((4, 16, 512), BF)
+
+    pl.semaphore_wait(barrier, len(peers))
+
+    a2a = []
+    for d in (1, 2, 3):
+        a2a.append(send(xf.at[te, lax.rem(px + d, NX)], xq.at[te, 3 - d], a_s.at[3 - d], ar.at[3 - d], at_x(d)))
+    for c in a2a:
+        c.start()
+    tok_y = [send(xf.at[te], xf.at[te], ts.at[d - 1], tr.at[d - 1], at_y(d)) for d in (1, 2, 3)]
+    for c in tok_y:
+        c.start()
+    tok_core = [send(xf.at[te], xf.at[te], tcs.at[0], tcr.at[0], other)]
+    tok_core[0].start()
+
+    load_cot.wait()
+    parts = [pl.ds(i * 64, 64) for i in range(4)]
+    cx = []
+
+    def send_part(i):
+        at = len(cx)
+        cx.append(send(cotv.at[0, parts[i]], cotv.at[3, parts[i]], xs.at[at], xr.at[at], at_x(1)))
+        cx[-1].start()
+        at += 1
+        cx.append(send(cotv.at[0, parts[3 - i]], cotv.at[1, parts[3 - i]], xs.at[at], xr.at[at], at_x(3)))
+        cx[-1].start()
+
+    send_part(0)
+    send_part(1)
 
     lane = lax.broadcasted_iota(jnp.int32, (1, 128), 1)
 
@@ -132,34 +161,6 @@
 
     lax.fori_loop(0, 8, place_step, 0)
     place_rows(8, 2)
-
-    pl.semaphore_wait(barrier, len(peers))
-
-    a2a = []
-    for d in (1, 2, 3):
-        a2a.append(send(xf.at[te, lax.rem(px + d, NX)], xq.at[te, 3 - d], a_s.at[3 - d], ar.at[3 - d], at_x(d)))
-    for c in a2a:
-        c.start()
-    tok_y = [send(xf.at[te], xf.at[te], ts.at[d - 1], tr.at[d - 1], at_y(d)) for d in (1, 2, 3)]
-    for c in tok_y:
-        c.start()
-    tok_core = [send(xf.at[te], xf.at[te], tcs.at[0], tcr.at[0], other)]
-    tok_core[0].start()
-
-    load_cot.wait()
-    parts = [pl.ds(i * 64, 64) for i in range(4)]
-    cx = []
-
-    def send_part(i):
-        at = len(cx)
-        cx.append(send(cotv.at[0, parts[i]], cotv.at[3, parts[i]], xs.at[at], xr.at[at], at_x(1)))
-        cx[-1].start()
-        at += 1
-        cx.append(send(cotv.at[0, parts[3 - i]], cotv.at[1, parts[3 - i]], xs.at[at], xr.at[at], at_x(3)))
-        cx[-1].start()
-
-    send_part(0)
-    send_part(1)
 
     low = lax.broadcasted_iota(jnp.int32, (64, 128), 1) < 64
 
@@ -239,16 +240,18 @@
     b_core = send(bp.at[pl.ds((1 - pc) * 4, 4)], bcore, bcs.at[0], bcr.at[0], other)
     b_core.start()
 
+    for c in cx[:4]:
+        c.wait_recv()
     fwd = []
-    for i in (0, 1):
-        cx[2 * i].wait_recv()
-        fwd.append(send(cotv.at[3, parts[i]], cotv.at[2, parts[i]], xs.at[8 + 2 * i], xr.at[8 + 2 * i], at_x(1)))
-        fwd[-1].start()
-        cx[2 * i + 1].wait_recv()
-        fwd.append(
-            send(cotv.at[1, parts[3 - i]], cotv.at[2, parts[3 - i]], xs.at[9 + 2 * i], xr.at[9 + 2 * i], at_x(3))
-        )
-        fwd[-1].start()
+
+    def forward(columns):
+        for up in (True, False):
+            rel, rows, to = (3, pl.ds(0, 128), at_x(1)) if up else (1, pl.ds(128, 128), at_x(3))
+            at = 8 + len(fwd)
+            fwd.append(send(cotv.at[rel, rows, columns], cotv.at[2, rows, columns], xs.at[at], xr.at[at], to))
+            fwd[-1].start()
+
+    forward(pl.ds(0, EARLY))
 
     relay(xq, xq_y, xq_core, qcs, qcr)
 
@@ -264,9 +267,8 @@
         hidden_tile(pl.multiple_of(n * 256, 256), 256)
         return carry
 
-    lax.fori_loop(0, 8, hidden_step, 0)
+    lax.fori_loop(0, 4, hidden_step, 0)
     lax.fori_loop(0, 7, pick_step, 0)
-    hidden_tile(2048, 128)
 
     b_core.wait_recv()
     b_y = []
@@ -310,50 +312,55 @@
     lax.fori_loop(0, 8, outer_step, 0)
     outer_tile(2048, 128)
 
-    for c in fwd:
-        c.wait_recv()
-
-    def square_last(i, carry):
-        rows = pl.ds(pl.multiple_of(i * 64, 64), 64)
-        cotv[2, rows, :] = square(cotv[2, rows, :])
-        return carry
-
-    lax.fori_loop(0, 4, square_last, 0)
-
-    def chunks(da, db):
+    for c in fwd[:2]:
+        c.wait_send()
+    forward(pl.ds(EARLY, COLS - EARLY))
+
+    def square_last(start, width):
+        def step(i, carry):
+            at = (2, pl.ds(pl.multiple_of(i * 64, 64), 64), pl.ds(start, width))
+            cotv[at] = square(cotv[at])
+            return carry
+
+        lax.fori_loop(0, 4, step, 0)
+
+    def rearrange(g, da, db, start, width):
         at = [lax.rem(pz + d, NZ) for d in (da, db)]
-
-        def rearrange(start, width):
-            lhs = jnp.concatenate([x2t[z, :, :, pl.ds(3 * T, T)].reshape(128, T) for z in at], axis=0)
-            last = dot(lhs, cotv[2, :, pl.ds(start, width)])
-            for side in range(2):
-                whole = acc[at[side], :, pl.ds(start, width)] + last[side * 128 : side * 128 + 128]
-                for pair in range(width // 128):
-                    o = whole[:, pair * 128 : pair * 128 + 128].reshape(8, 2, 8, 128)
-                    p0 = o[:, 0].reshape(64, 128)
-                    p1 = o[:, 1].reshape(64, 128)
-                    a = jnp.where(low, p0, pltpu.roll(p1, 64, 1))
-                    b = jnp.where(low, pltpu.roll(p0, 64, 1), p1)
-                    slot = start // 64 + pair * 2
-                    gbuf[slot, :, side * 128 : side * 128 + 128] = a.astype(BF)
-                    gbuf[slot + 1, :, side * 128 : side * 128 + 128] = b.astype(BF)
-
+        lhs = jnp.concatenate([x2t[z, :, :, pl.ds(3 * T, T)].reshape(128, T) for z in at], axis=0)
+        last = dot(lhs, cotv[2, :, pl.ds(start, width)])
+        for side in range(2):
+            whole = acc[at[side], :, pl.ds(start, width)] + last[side * 128 : side * 128 + 128]
+            for pair in range(width // 128):
+                o = whole[:, pair * 128 : pair * 128 + 128].reshape(8, 2, 8, 128)
+                p0 = o[:, 0].reshape(64, 128)
+                p1 = o[:, 1].reshape(64, 128)
+                a = jnp.where(low, p0, pltpu.roll(p1, 64, 1))
+                b = jnp.where(low, pltpu.roll(p0, 64, 1), p1)
+                slot = start // 64 + pair * 2
+                gbuf[g, slot, :, side * 128 : side * 128 + 128] = a.astype(BF)
+                gbuf[g, slot + 1, :, side * 128 : side * 128 + 128] = b.astype(BF)
+
+    def chunks(g, da, db, columns, windows_of):
         def rearrange_step(n, carry):
-            rearrange(pl.multiple_of(n * 256, 256), 256)
+            rearrange(g, da, db, pl.multiple_of(n * 256, 256), 256)
             return carry
 
-        lax.fori_loop(0, 8, rearrange_step, 0, unroll=2)
-        rearrange(2048, 128)
+        first, end = columns
+        lax.fori_loop((first + 255) // 256, end // 256, rearrange_step, 0, unroll=2)
+        if first % 256:
+            rearrange(g, da, db, first, 128)
+        if end % 256:
+            rearrange(g, da, db, end - 128, 128)
 
         def window(i, carry):
-            rhs = jnp.concatenate([gbuf[slots[(i * 4 + g) * 16]] for g in range(4)], axis=0)
+            rhs = jnp.concatenate([gbuf[g, slots[(i * 4 + k) * 16]] for k in range(4)], axis=0)
             rows = pl.ds(pl.multiple_of(i * 64, 64), 64)
             out = dot(pick[rows, :], rhs).astype(BF)
             y[da, rows, :] = out[:, :128]
             y[db, rows, :] = out[:, 128:]
             return carry
 
-        lax.fori_loop(0, 14, window, 0, unroll=7)
+        lax.fori_loop(*windows_of, window, 0, unroll=7)
 
     rows_of = [pl.ds(i * QUARTER, QUARTER) for i in range(4)]
     sent = {}
@@ -374,32 +381,53 @@
         for h in parts_of:
             z_step(up, step, h)
 
-    chunks(4, 3)
-    z_steps(True, 0, (0, 1))
-    z_steps(False, 0, (3, 2))
-    z_steps(True, 1, (2, 3))
-    chunks(5, 2)
-    z_steps(False, 1, (1, 0))
-    z_steps(True, 1, (0, 1))
-    z_steps(False, 1, (3, 2))
-    chunks(6, 1)
-    z_steps(True, 2, (2, 3))
-    z_steps(False, 2, (1, 0))
-    z_steps(True, 2, (0, 1))
-    z_steps(False, 2, (3, 2))
-    chunks(7, 0)
-    z_steps(True, 3, (2, 3))
-    z_steps(False, 3, (1, 0))
-    z_steps(True, 3, (0, 1))
-    z_steps(False, 3, (3, 2))
+    early, late, every = (0, EARLY), (EARLY, COLS), (0, COLS)
+    half_a, half_b, both = (0, 7), (7, 14), (0, 14)
+    for c in fwd[:2]:
+        c.wait_recv()
+    square_last(0, EARLY)
+    chunks(0, 4, 3, early, half_a)
+    z_step(True, 0, 0)
+    z_step(False, 0, 1)
+    z_step(True, 1, 1)
+    chunks(1, 5, 2, early, half_a)
+    z_step(False, 1, 0)
+    for c in fwd[2:]:
+        c.wait_recv()
+    square_last(EARLY, COLS - EARLY)
+    chunks(0, 4, 3, late, half_b)
+    z_step(True, 0, 2)
+    z_step(False, 0, 3)
+    z_step(True, 1, 3)
+    chunks(1, 5, 2, late, half_b)
+    z_step(False, 1, 2)
+    z_step(True, 1, 0)
+    z_step(False, 1, 1)
+    z_step(True, 1, 2)
+    z_step(False, 1, 3)
+    chunks(0, 6, 1, every, both)
+    for h in (1, 0, 3, 2):
+        z_step(True, 2, h)
+        z_step(False, 2, h ^ 1)
+    chunks(1, 7, 0, every, both)
+    lax.fori_loop(4, 6, hidden_step, 0)
+    for h in (1, 0, 3, 2):
+        z_step(True, 3, h)
+        z_step(False, 3, h ^ 1)
+    lax.fori_loop(6, 8, hidden_step, 0)
+    hidden_tile(2048, 128)
+    store_hid = pltpu.make_async_copy(hid, hid_out, loc_sem.at[0])
+    store_hid.start()
 
     total = bp[pc * 4 + py].astype(F32) + bcore[py].astype(F32)
     for d in (1, 2, 3):
         b_y[d - 1].wait_recv()
         total = total + by[d - 1].astype(F32)
     grads[...] = dot(perm, total.astype(BF)).T.astype(BF)
-
-    for h in (2, 1, 0, 3):
+    store_grads = pltpu.make_async_copy(grads, grads_out, loc_sem.at[1])
+    store_grads.start()
+
+    for h in (1, 0, 3, 2):
         sent[(True, 3, h)].wait_recv()
         sent[(False, 3, h)].wait_recv()
         value = (
@@ -409,14 +437,30 @@
         )
         curv[rows_of[h], :] = value * (1.0 / 8192.0)
 
-    for c in a2a + tok_y + tok_core + cx[4:] + xq_y + xq_core + fwd + [b_core] + b_y + list(sent.values()):
+    store_hid.wait()
+    store_grads.wait()
+    for c in a2a + tok_y + tok_core + cx[4:] + xq_y + xq_core + fwd[2:] + [b_core] + b_y + list(sent.values()):
         c.wait_send()
 
 
-def place_kernel(a, b, c, oa, ob, oc):
-    oa[...] = a[...]
-    ob[...] = b[...]
-    oc[...] = c[...]
+def place_kernel(a, b, c, oa, ob, oc, va, vb, vc, sem):
+    pieces = []
+    for src, mid, dst, cuts in ((a, va, oa, 4), (c, vc, oc, 2), (b, vb, ob, 1)):
+        size = src.shape[0] // cuts
+        for i in range(cuts):
+            rows = pl.ds(i * size, size)
+            at = len(pieces)
+            pieces.append((
+                pltpu.make_async_copy(src.at[rows], mid.at[rows], sem.at[at]),
+                pltpu.make_async_copy(mid.at[rows], dst.at[rows], sem.at[7 + at]),
+            ))
+    for load, _ in pieces:
+        load.start()
+    for load, store in pieces:
+        load.wait()
+        store.start()
+    for _, store in pieces:
+        store.wait()
 
 
 def tables(block_rows, block_slots):
@@ -439,8 +483,10 @@
             jax.ShapeDtypeStruct((KEPT, 128), F32),
         ),
         in_specs=[vm, hb, hb, vm, sm],
-        out_specs=(vm, vm, vm),
+        out_specs=(hb, hb, vm),
         scratch_shapes=[
+            pltpu.VMEM((T, COLS), BF),
+            pltpu.VMEM((T, F), BF),
             pltpu.SMEM((SLOTS,), jnp.int32),
             pltpu.VMEM((KEPT, 256), BF),
             pltpu.VMEM((SLOTS * 64, 256), BF),
@@ -452,7 +498,7 @@
             pltpu.VMEM((8, 3, T, 128), BF),
             pltpu.VMEM((NZ, 8, 16, 4 * T), BF),
             pltpu.VMEM((NZ, 128, COLS), F32),
-            pltpu.VMEM((SLOTS, 64, 256), BF),
+            pltpu.VMEM((2, SLOTS, 64, 256), BF),
             pltpu.VMEM((8, KEPT, 128), BF),
             pltpu.VMEM((4, KEPT, 128), BF),
             pltpu.VMEM((4, KEPT, 128), BF),
@@ -480,8 +526,9 @@
     place = pl.pallas_call(
         place_kernel,
         out_shape=[jax.ShapeDtypeStruct(o.shape, o.dtype) for o in outs],
-        in_specs=[vm] * 3,
-        out_specs=[vm] * 3,
+        in_specs=[hb] * 3,
+        out_specs=[hb] * 3,
+        scratch_shapes=[pltpu.VMEM(o.shape, o.dtype) for o in outs] + [sem((14,))],
     )
     return tuple(place(*outs))
 

time: 78.4 us -> 76.2 us (0.972)
  Pallas kernels: 75.7 us -> 73.5 us
    pallas_call x1, Pallas kernels: 73 us -> 71.2 us  [body(): call(tokens, cotangent, weight_blocks.reshape(GROUPS, 16, 4096), window,...]
where the time goes in v3:
time: 76.2 us; the launch traced here: 76 us
  Pallas kernels  73.5 us (96%)
  local copies, waits for them, and re-layouts  1.12 us (1%)
    pallas_call x1, Pallas kernels, body(): call(tokens, cotangent, weight_blocks.reshape(GROUPS, 16, 4096), window,...  71.2 us
    pallas_call x1, Pallas kernels, body(): return tuple(place(*outs))  2.3 us

profile of v3, /device:TPU:8, one launch (start us, length us, event | category | flops | bytes accessed | tf_op | source)
XLA Modules:
  0.0 76.0 jit_solution(5220621907907317920)
XLA Ops:
  0.6 0.7 multiply_add_fusion
  1.3 0.1 pad_slice_fusion
  1.4 0.1 slice.63
  1.5 0.1 slice.59
  1.6 0.1 slice.61
  1.6 0.1 slice.57
  1.7 0.8 concatenate.3.windows
  2.5 71.2 %shard_map.76 = (bf16[256,2176]{1,0:T(8,128)(2,1)}, bf16[256,512]{1,0:T(8,128)(2,1)}, f32[896,128]{1,0:T(8,128)}) custom-call(bf16[256,512]{1,0:T(8,128)(2,1)} %tok.1, bf16[256,2176]{1,0:T(8,128)(2,1)} %cot_hbm.1, bf16[56,16,4096]{2,1,0:T(8,128)(2,1)} %bitcast.1, s32[60,128]{1,0:T(8,128)} %concatenate.3.windows, s32[896]{0:T(1024)} %slots.1), custom_call_target="tpu_custom_call" | custom-call | flops 14000000000 | bytes 12000000 | tf_op jit(solution)/shard_map/pallas_call | solution.py:525
  73.7 2.3 %shard_map.77 = (bf16[256,2176]{1,0:T(8,128)(2,1)}, bf16[256,512]{1,0:T(8,128)(2,1)}, f32[896,128]{1,0:T(8,128)}) custom-call(bf16[256,2176]{1,0:T(8,128)(2,1)} %get-tuple-element.6.a, bf16[256,512]{1,0:T(8,128)(2,1)} %get-tuple-element.7.b, f32[896,128]{1,0:T(8,128)} %get-tuple-element.8.c), custom_call_target="tpu_custom_call" | custom-call | tf_op jit(solution)/shard_map/pallas_call | solution.py:533

commit v4 on v3

--- a/solution.py
+++ b/solution.py
@@ -267,7 +267,7 @@
         hidden_tile(pl.multiple_of(n * 256, 256), 256)
         return carry
 
-    lax.fori_loop(0, 4, hidden_step, 0)
+    lax.fori_loop(0, 2, hidden_step, 0)
     lax.fori_loop(0, 7, pick_step, 0)
 
     b_core.wait_recv()
@@ -410,11 +410,11 @@
         z_step(True, 2, h)
         z_step(False, 2, h ^ 1)
     chunks(1, 7, 0, every, both)
-    lax.fori_loop(4, 6, hidden_step, 0)
+    lax.fori_loop(2, 5, hidden_step, 0)
     for h in (1, 0, 3, 2):
         z_step(True, 3, h)
         z_step(False, 3, h ^ 1)
-    lax.fori_loop(6, 8, hidden_step, 0)
+    lax.fori_loop(5, 8, hidden_step, 0)
     hidden_tile(2048, 128)
     store_hid = pltpu.make_async_copy(hid, hid_out, loc_sem.at[0])
     store_hid.start()

time: 76.2 us -> 76.9 us (level)
  Pallas kernels: 73.5 us -> 74.3 us
where the time goes in v4:
time: 76.9 us; the launch traced here: 76.7 us
  Pallas kernels  74.3 us (97%)
  local copies, waits for them, and re-layouts  1.12 us (1%)
    pallas_call x1, Pallas kernels, body(): call(tokens, cotangent, weight_blocks.reshape(GROUPS, 16, 4096), window,...  72 us
    pallas_call x1, Pallas kernels, body(): return tuple(place(*outs))  2.3 us

profile of v4, /device:TPU:8, one launch (start us, length us, event | category | flops | bytes accessed | tf_op | source)
XLA Modules:
  0.0 76.7 jit_solution(5826580492509678139)
XLA Ops:
  0.6 0.7 multiply_add_fusion
  1.3 0.1 pad_slice_fusion
  1.4 0.1 slice.63
  1.5 0.1 slice.59
  1.6 0.1 slice.61
  1.6 0.1 slice.57
  1.7 0.8 concatenate.3.windows
  2.5 72.0 %shard_map.76 = (bf16[256,2176]{1,0:T(8,128)(2,1)}, bf16[256,512]{1,0:T(8,128)(2,1)}, f32[896,128]{1,0:T(8,128)}) custom-call(bf16[256,512]{1,0:T(8,128)(2,1)} %tok.1, bf16[256,2176]{1,0:T(8,128)(2,1)} %cot_hbm.1, bf16[56,16,4096]{2,1,0:T(8,128)(2,1)} %bitcast.1, s32[60,128]{1,0:T(8,128)} %concatenate.3.windows, s32[896]{0:T(1024)} %slots.1), custom_call_target="tpu_custom_call" | custom-call | flops 14000000000 | bytes 12000000 | tf_op jit(solution)/shard_map/pallas_call | solution.py:525
  74.4 2.3 %shard_map.77 = (bf16[256,2176]{1,0:T(8,128)(2,1)}, bf16[256,512]{1,0:T(8,128)(2,1)}, f32[896,128]{1,0:T(8,128)}) custom-call(bf16[256,2176]{1,0:T(8,128)(2,1)} %get-tuple-element.6.a, bf16[256,512]{1,0:T(8,128)(2,1)} %get-tuple-element.7.b, f32[896,128]{1,0:T(8,128)} %get-tuple-element.8.c), custom_call_target="tpu_custom_call" | custom-call | tf_op jit(solution)/shard_map/pallas_call | solution.py:533
